TPU v7x, 128 devices: a whole 4x4x4 slice. The times are simulated.
128 devices in a mesh: dp: 16 (over x, y), red: 8 (over z, core).
Axes of the slice: x: 4, y: 4, z: 4, core: 2. Of those that a mesh axis runs over, the one named last changes fastest.
Arguments:
- frames: bfloat16 [2048, 48, 1536], P(('dp', 'red')), may hold values from -36 to 36
- cotangent: bfloat16 [2048, 48, 1536], P(('dp', 'red')), may hold values from -6 to 6
- w_in: bfloat16 [1536, 3072], P('red'), may hold values from -0.15625 to 0.15625
- kernel: float32 [31, 1536], replicated, may hold values from -1 to 1
- gain: float32 [1536], replicated, may hold values from 0.25 to 1.75
- lengths: int32 [2048], replicated, may hold values from 1 to 47, as said below
Outputs:
- module_output: bfloat16 [2048, 48, 1536], P(('dp', 'red'))
- frame_gradient: bfloat16 [2048, 48, 1536], P(('dp', 'red'))
- grad_w_in: float32 [1536, 3072], P('red')
- grad_kernel: float32 [31, 1536], replicated
- grad_gain: float32 [1536], replicated
Inputs may be any that keep to these rules, and one draw needn't show every extreme that they name: The slots of each device, in order, form 16 groups of 1 slots. The q-th slot of group j on the device with dp index i and red index r and the q-th slot of group j on the device with dp index (2 j + 1 - i) mod 16 and the same red index have lengths that sum to exactly 48. The slots of dp index 0 all hold at least three quarters of 48 frames, rounded up.
All inputs are finite; a program needn't handle non-finite values.
Results may differ from a plain program's by a relative error of at most 0.0054.
Values may be sent and summed in bfloat16 or wider, within the bound.
A program may use at most 128 MiB of HBM per device.

v0:
```python
import jax
import jax.numpy as jnp
from jax import lax
from jax.sharding import PartitionSpec as P

EPSILON = 1e-05


def normalize(widened_frames):
    center = widened_frames - jnp.mean(widened_frames, axis=-1, keepdims=True)
    inv_std = lax.rsqrt(jnp.mean(center * center, axis=-1, keepdims=True) + EPSILON)
    return (center * inv_std, inv_std)


def block_pass(frames, cotangent, valid_frame_mask, segment, weights, kernel, gain):
    row_count, length, model_width = frames.shape
    tap_count = kernel.shape[0]
    reach = tap_count // 2
    widened_frames = frames.astype(jnp.float32)
    normed, inv_std = normalize(widened_frames)
    scaled = (normed * gain).astype(jnp.bfloat16)
    flat_in = scaled.reshape(row_count * length, model_width)
    hidden = jnp.dot(flat_in, weights, preferred_element_type=jnp.float32)
    hidden = hidden.reshape(row_count, length, 2 * model_width)
    value_portion = hidden[..., :model_width]
    gate_sigmoid = jax.nn.sigmoid(hidden[..., model_width:])
    frame_validity = valid_frame_mask.astype(jnp.float32)[..., None]
    gated_linear_output = value_portion * gate_sigmoid * frame_validity
    padded = jnp.pad(gated_linear_output, ((0, 0), (reach, reach), (0, 0)))
    seg_pad = jnp.pad(segment, ((0, 0), (reach, reach)), constant_values=-1)
    convolved_frames = jnp.zeros_like(gated_linear_output)
    for offset in range(tap_count):
        window = padded[:, offset : offset + length]
        same_seg = (seg_pad[:, offset : offset + length] == segment).astype(jnp.float32)[..., None]
        convolved_frames = convolved_frames + kernel[offset] * (window * same_seg)
    swish_activation = jax.nn.sigmoid(convolved_frames)
    module_output = (
        (widened_frames + convolved_frames * swish_activation) * frame_validity
    ).astype(jnp.bfloat16)
    incoming_gradient = cotangent.astype(jnp.float32) * frame_validity
    grad_conv = incoming_gradient * (
        swish_activation * (1.0 + convolved_frames * (1.0 - swish_activation))
    )
    grad_pad = jnp.pad(grad_conv, ((0, 0), (reach, reach), (0, 0)))
    gated_linear_gradient = jnp.zeros_like(gated_linear_output)
    kernel_terms = []
    for offset in range(tap_count):
        window = padded[:, offset : offset + length]
        same_seg = (seg_pad[:, offset : offset + length] == segment).astype(jnp.float32)[..., None]
        kernel_terms.append(jnp.sum(grad_conv * window * same_seg, axis=(0, 1)))
        back_start = 2 * reach - offset
        back_same = (seg_pad[:, back_start : back_start + length] == segment).astype(jnp.float32)[
            ..., None
        ]
        gated_linear_gradient = gated_linear_gradient + kernel[offset] * (
            grad_pad[:, back_start : back_start + length] * back_same
        )
    gated_linear_gradient = gated_linear_gradient * frame_validity
    grad_hidden = jnp.concatenate(
        [
            gated_linear_gradient * gate_sigmoid,
            gated_linear_gradient * value_portion * gate_sigmoid * (1.0 - gate_sigmoid),
        ],
        axis=-1,
    ).astype(jnp.bfloat16)
    flat_grad = grad_hidden.reshape(row_count * length, 2 * model_width)
    grad_scaled = lax.dot_general(
        flat_grad, weights, (((1,), (1,)), ((), ())), preferred_element_type=jnp.float32
    )
    grad_scaled = grad_scaled.reshape(row_count, length, model_width)
    gain_term = jnp.sum(grad_scaled * normed, axis=(0, 1))
    grad_normed = grad_scaled * gain
    frame_gradient = incoming_gradient + inv_std * (
        grad_normed
        - jnp.mean(grad_normed, axis=-1, keepdims=True)
        - normed * jnp.mean(grad_normed * normed, axis=-1, keepdims=True)
    )
    frame_gradient = (frame_gradient * frame_validity).astype(jnp.bfloat16)
    return (module_output, frame_gradient, flat_in, flat_grad, jnp.stack(kernel_terms), gain_term)


def local(frames, cotangent, w_in, kernel, gain, lengths):
    dp_size = lax.axis_size("dp")
    red_size = lax.axis_size("red")
    dp_index = lax.axis_index("dp")
    red_index = lax.axis_index("red")
    local_utts, length, model_width = frames.shape
    weights = lax.all_gather(w_in, "red", axis=0, tiled=True)
    positions = jnp.arange(length, dtype=jnp.int32)
    by_owner = lengths.reshape(dp_size, red_size, local_utts)
    own_lengths = lax.dynamic_slice(by_owner, (dp_index, red_index, 0), (1, 1, local_utts)).reshape(
        local_utts
    )
    valid_frame_mask = positions[None, :] < own_lengths[:, None]
    segment = jnp.where(valid_frame_mask, 0, 1).astype(jnp.int32)
    module_output, frame_gradient, flat_in, flat_grad, kernel_part, gain_part = block_pass(
        frames, cotangent, valid_frame_mask, segment, weights, kernel, gain
    )
    grad_scale = lax.rsqrt(jnp.sum(lengths).astype(jnp.float32))
    block_rows = model_width // (dp_size * red_size)
    ordered = flat_in.reshape(-1, red_size, dp_size, block_rows)
    ordered = jnp.transpose(ordered, (0, 2, 1, 3)).reshape(-1, model_width)
    owned_rows = lax.psum_scatter(
        lax.dot_general(
            ordered, flat_grad, (((0,), (0,)), ((), ())), preferred_element_type=jnp.float32
        ),
        ("dp", "red"),
        scatter_dimension=0,
        tiled=True,
    )
    grad_weights = lax.all_gather(owned_rows, "dp", axis=0, tiled=True)
    kernel_total, gain_total = lax.psum((kernel_part, gain_part), ("dp", "red"))
    return (
        module_output,
        frame_gradient,
        grad_weights * grad_scale,
        kernel_total * grad_scale,
        gain_total * grad_scale,
    )


def solution(mesh):
    placed = (
        P(("dp", "red"), None, None),
        P(("dp", "red"), None, None),
        P("red", None),
        P(),
        P(),
        P(),
    )
    return jax.shard_map(
        local,
        mesh=mesh,
        in_specs=placed,
        out_specs=(
            P(("dp", "red"), None, None),
            P(("dp", "red"), None, None),
            P("red", None),
            P(),
            P(),
        ),
        check_vma=False,
    )
```

profile of v0, /device:TPU:1, one launch (start us, length us, event | category | flops | bytes accessed | tf_op | source)
XLA Modules:
  0.0 923.5 jit_solution(477016552205187638)
XLA Ops:
  14.4 8.3 copy.13
  22.7 10.7 %reshape_reshape.3 = bf16[768,8,16,12]{0,3,2,1:T(8,128)(2,1)} reshape(bf16[16,48,1536]{1,0,2:T(8,128)(2,1)} %copy.13) | data formatting | bytes 4718592 | tf_op jit(solution)/shard_map/reshape;reshape | solution.py:101
  43.8 23.9 %all-gather.4.cloned.1.call-done = bf16[1536,3072]{1,0:T(8,128)(2,1)} async-done(((bf16[192,3072]{1,0:T(8,128)(2,1)}), bf16[1536,3072]{1,0:T(8,128)(2,1)}) %all-gather.4.cloned.1.call-update) | async-done | bytes 9437200 | tf_op jit(solution)/shard_map/all_gather | solution.py:88
  67.7 10.8 %fusion.3 = f32[16,48,3072]{2,1,0:T(8,128)S(1)} fusion(bf16[16,48,1536]{2,1,0:T(8,128)(2,1)} %fusion.11, bf16[1536,3072]{1,0:T(8,128)(2,1)} %all-gather.4.cloned.1.call-done), kind=kOutput, calls=%fused_computation.62 | convolution fusion | flops 7247757312 | bytes 21233664 | tf_op jit(solution)/shard_map/dot_general | solution.py:23
  82.6 49.2 %multiply_reduce_fusion = (f32[1536]{0:T(1024)}, f32[1536]{0:T(1024)}, f32[1536]{0:T(1024)}, f32[1536]{0:T(1024)}, f32[1536]{0:T(1024)}, /*index=5*/f32[1536]{0:...) fusion(f32[16,48,1536]{2,1,0:T(8,128)S(1)} %multiply_multiply_f, ...), kind=kLoop, calls=%fused_computation.186 | loop fusion | flops 150981120 | bytes 16856064 | tf_op jit(solution)/shard_map/reduce_sum | solution.py:50
  132.0 28.6 %multiply_convert_fusion.1 = (bf16[16,48,1536]{2,1,0:T(8,128)(2,1)S(1)}, f32[16,48,1536]{2,1,0:T(8,128)}) fusion(f32[16,48,3072]{2,1,0:T(8,128)} %copy-done.3, f32[16,48]{1,0:T(8,128)S(1)} %get-tuple-element.106, f32[16,48]{1,0:T(8,128)S(1)} %get-tuple-element.76, f32[1536]{0:T(1024)} %copy-done.57, f32[16,48]{1,0:T(8,128)S(1)} %get-tuple-element.77, ...), kind=kLoop, calls=%fused_computation.218 | loop fusion | flops 114425856 | bytes 16800768 | tf_op jit(solution)/shard_map/convert.4
  160.6 6.9 multiply_convert_fusion
  168.9 10.8 %fusion.119 = f32[1536,3072]{1,0:T(8,128)} fusion(bf16[768,1536]{0,1:T(8,128)(2,1)S(1)} %copy-done.8, bf16[768,1536]{1,0:T(8,128)(2,1)S(1)} %bitcast.24, bf16[768,1536]{1,0:T(8,128)(2,1)S(1)} %bitcast.23), kind=kOutput, calls=%fused_computation.182 | convolution fusion | flops 7257194496 | bytes 25952256 | tf_op jit(solution)/shard_map/dot_general | solution.py:104
  179.8 359.8 %fusion = f32[16,3072]{1,0:T(8,128)S(1)} fusion(f32[1536,3072]{1,0:T(8,128)} %fusion.119), kind=kCustom, calls=%all-reduce-scatter | all-reduce-scatter fusion | flops 6291457 | bytes 19070976
  552.0 15.3 %collective-permute-start.22 = (f32[16,3072]{1,0:T(8,128)S(1)}, f32[16,3072]{1,0:T(8,128)S(1)}, u32[]{:S(2)}, u32[]{:S(2)}) collective-permute-start(f32[16,3072]{1,0:T(8,128)S(1)} %fusion), channel_id=1, source_target_pairs={{0,23},{1,24},{2,25},{3,26},{4,27},{5,28},{6,29},{7,30},{8,31},{9,... | collective-permute-start | bytes 589832
  567.3 6.4 collective-permute-start.21
  579.4 8.4 collective-permute-start.19
  589.8 5.9 collective-permute-start.17
  608.6 12.3 %collective-permute-start.13 = (f32[16,3072]{1,0:T(8,128)S(1)}, f32[16,3072]{1,0:T(8,128)S(1)}, u32[]{:S(2)}, u32[]{:S(2)}) collective-permute-start(f32[16,3072]{1,0:T(8,128)S(1)} %fusion), channel_id=1, source_target_pairs={{0,14},{1,15},{2,16},{3,17},{4,18},{5,19},{6,20},{7,21},{8,22},{9,... | collective-permute-start | bytes 589832
  620.9 10.3 %collective-permute-start.12 = (f32[16,3072]{1,0:T(8,128)S(1)}, f32[16,3072]{1,0:T(8,128)S(1)}, u32[]{:S(2)}, u32[]{:S(2)}) collective-permute-start(f32[16,3072]{1,0:T(8,128)S(1)} %fusion), channel_id=1, source_target_pairs={{0,13},{1,14},{2,15},{3,16},{4,17},{5,18},{6,19},{7,20},{8,21},{9,... | collective-permute-start | bytes 589832
  631.2 14.7 %collective-permute-start.11 = (f32[16,3072]{1,0:T(8,128)S(1)}, f32[16,3072]{1,0:T(8,128)S(1)}, u32[]{:S(2)}, u32[]{:S(2)}) collective-permute-start(f32[16,3072]{1,0:T(8,128)S(1)} %fusion), channel_id=1, source_target_pairs={{0,12},{1,13},{2,14},{3,15},{4,16},{5,17},{6,18},{7,19},{8,20},{9,... | collective-permute-start | bytes 589832
  647.3 26.0 %multiply_reduce_fusion.9 = (f32[1536]{0:T(1024)S(1)}, f32[1536]{0:T(1024)S(1)}, f32[1536]{0:T(1024)S(1)}, f32[1536]{0:T(1024)S(1)}, f32[1536]{0:T(1024)S(1)}, /...) fusion(f32[16,48,1536]{2,1,0:T(8,128)} %copy-done.1, f32[16,48,1536]{2,1,0:T(8,128)} %copy-done, ...), kind=kLoop, calls=%fused_computation.195 | loop fusion | flops 30657024 | bytes 9517056 | tf_op jit(solution)/shard_map/reduce_sum | solution.py:50
  687.9 9.0 multiply_reduce_fusion.18
  697.0 6.7 collective-permute-start.4
  722.4 84.8 %concatenate.17 = f32[524,3072]{1,0:T(8,128)} concatenate(f32[12,3072]{1,0:T(8,128)S(1)} %collective-permute-done.31, f32[16,3072]{1,0:T(8,128)S(1)} %collective-permute-done.30, f32[16,3072]{1,0:T(8,128)} %copy-done.9, f32[16,3072]{1,0:T(8,128)} %copy-done.10, f32[16,3072]{1,0:T(8,128)} %copy-done.11, f32[16,3072]{1,0:T(8,128)} %copy-done.12, f32[16,3072]{1,0:T(8,128)} %copy-done.13, ...), dimensions={0} | concatenate | bytes 12877824
  808.9 14.3 %fusion.18 = (f32[1536]{0:T(1024)S(1)}, f32[16,48]{1,0:T(8,128)S(1)}, f32[16,48]{1,0:T(8,128)S(1)}, f32[16,48,1536]{2,1,0:T(8,128)}) fusion(bf16[16,48,1536]{2,1,0:T(8,128)(2,1)S(1)} %copy-done.4, f32[16,48]{1,0:T(8,128)S(1)} %copy-done.60, f32[16,48]{1,0:T(8,128)S(1)} %copy-done.52, f32[1536]{0:T(1024)S(1)} %copy-done.62, ...), kind=kOutput, calls=%fused_computation.80 | convolution fusion | flops 7267808256 | bytes 21258240 | tf_op jit(solution)/shard_map/dot_general | solution.py:67
  823.2 63.9 %psum.15 = f32[1536]{0:T(1024)S(1)} all-reduce(f32[1536]{0:T(1024)S(1)} %get-tuple-element.36), channel_id=1, replica_groups=mesh['dp'=16,'red'=8] {'dp','red'}, use_global_device_ids=true, to_apply=%region_39.40 | all-reduce | flops 1536 | bytes 12288 | tf_op jit(solution)/shard_map/psum | solution.py:112
  887.7 7.8 fusion.17
  897.2 12.9 %all-gather.6.cloned.1.call-done = f32[16,12,3072]{2,1,0:T(8,128)} async-done(((f32[1,12,3072]{2,1,0:T(8,128)}), f32[16,12,3072]{2,1,0:T(8,128)}) %all-gather.6.cloned.1.call-update) | async-done | bytes 2359312 | tf_op jit(solution)/shard_map/all_gather | solution.py:111
  (272 shorter events, 99.6 us)
Async XLA Ops:
  7.2 60.5 %all-gather.4.cloned.1.call-start = ((), (), s32[]{:S(2)}) async-start(), calls=%async_computation | async-start | bytes 10616832 | tf_op jit(solution)/shard_map/all_gather | solution.py:88
  7.9 887.6 %all-reduce.7.cloned.1.call-start = ((), (), s32[]{:S(2)}) async-start(), calls=%async_computation.1 | async-start | bytes 393216 | tf_op jit(solution)/shard_map/psum | solution.py:112
  547.5 26.2 %collective-permute-start.25 = (f32[16,3072]{1,0:T(8,128)S(1)}, f32[16,3072]{1,0:T(8,128)S(1)}, u32[]{:S(2)}, u32[]{:S(2)}) collective-permute-start(f32[16,3072]{1,0:T(8,128)S(1)} %fusion), channel_id=1, source_target_pairs={{0,26},{1,27},{2,28},{3,29},{4,30},{5,31},{6,32},{7,33},{8,34},{9,... | collective-permute-start | bytes 589832
  548.8 30.6 %collective-permute-start.24 = (f32[16,3072]{1,0:T(8,128)S(1)}, f32[16,3072]{1,0:T(8,128)S(1)}, u32[]{:S(2)}, u32[]{:S(2)}) collective-permute-start(f32[16,3072]{1,0:T(8,128)S(1)} %fusion), channel_id=1, source_target_pairs={{0,25},{1,26},{2,27},{3,28},{4,29},{5,30},{6,31},{7,32},{8,33},{9,... | collective-permute-start | bytes 589832
  550.2 37.6 %collective-permute-start.23 = (f32[16,3072]{1,0:T(8,128)S(1)}, f32[16,3072]{1,0:T(8,128)S(1)}, u32[]{:S(2)}, u32[]{:S(2)}) collective-permute-start(f32[16,3072]{1,0:T(8,128)S(1)} %fusion), channel_id=1, source_target_pairs={{0,24},{1,25},{2,26},{3,27},{4,28},{5,29},{6,30},{7,31},{8,32},{9,... | collective-permute-start | bytes 589832
  552.0 37.8 %collective-permute-start.22 = (f32[16,3072]{1,0:T(8,128)S(1)}, f32[16,3072]{1,0:T(8,128)S(1)}, u32[]{:S(2)}, u32[]{:S(2)}) collective-permute-start(f32[16,3072]{1,0:T(8,128)S(1)} %fusion), channel_id=1, source_target_pairs={{0,23},{1,24},{2,25},{3,26},{4,27},{5,28},{6,29},{7,30},{8,31},{9,... | collective-permute-start | bytes 589832
  567.3 28.4 %collective-permute-start.21 = (f32[16,3072]{1,0:T(8,128)S(1)}, f32[16,3072]{1,0:T(8,128)S(1)}, u32[]{:S(2)}, u32[]{:S(2)}) collective-permute-start(f32[16,3072]{1,0:T(8,128)S(1)} %fusion), channel_id=1, source_target_pairs={{0,22},{1,23},{2,24},{3,25},{4,26},{5,27},{6,28},{7,29},{8,30},{9,... | collective-permute-start | bytes 589832
  573.7 24.0 %collective-permute-start.20 = (f32[16,3072]{1,0:T(8,128)S(1)}, f32[16,3072]{1,0:T(8,128)S(1)}, u32[]{:S(2)}, u32[]{:S(2)}) collective-permute-start(f32[16,3072]{1,0:T(8,128)S(1)} %fusion), channel_id=1, source_target_pairs={{0,21},{1,22},{2,23},{3,24},{4,25},{5,26},{6,27},{7,28},{8,29},{9,... | collective-permute-start | bytes 589832
  579.4 23.7 %collective-permute-start.19 = (f32[16,3072]{1,0:T(8,128)S(1)}, f32[16,3072]{1,0:T(8,128)}, u32[]{:S(2)}, u32[]{:S(2)}) collective-permute-start(f32[16,3072]{1,0:T(8,128)S(1)} %fusion), channel_id=1, source_target_pairs={{0,20},{1,21},{2,22},{3,23},{4,24},{5,25},{6,26},{7,27},{8,28},{9,... | collective-permute-start | bytes 589832
  589.8 31.1 %collective-permute-start.17 = (f32[16,3072]{1,0:T(8,128)S(1)}, f32[16,3072]{1,0:T(8,128)}, u32[]{:S(2)}, u32[]{:S(2)}) collective-permute-start(f32[16,3072]{1,0:T(8,128)S(1)} %fusion), channel_id=1, source_target_pairs={{0,18},{1,19},{2,20},{3,21},{4,22},{5,23},{6,24},{7,25},{8,26},{9,... | collective-permute-start | bytes 589832
  595.7 35.5 %collective-permute-start.16 = (f32[16,3072]{1,0:T(8,128)S(1)}, f32[16,3072]{1,0:T(8,128)}, u32[]{:S(2)}, u32[]{:S(2)}) collective-permute-start(f32[16,3072]{1,0:T(8,128)S(1)} %fusion), channel_id=1, source_target_pairs={{0,17},{1,18},{2,19},{3,20},{4,21},{5,22},{6,23},{7,24},{8,25},{9,... | collective-permute-start | bytes 589832
  597.7 48.2 %collective-permute-start.15 = (f32[16,3072]{1,0:T(8,128)S(1)}, f32[16,3072]{1,0:T(8,128)}, u32[]{:S(2)}, u32[]{:S(2)}) collective-permute-start(f32[16,3072]{1,0:T(8,128)S(1)} %fusion), channel_id=1, source_target_pairs={{0,16},{1,17},{2,18},{3,19},{4,20},{5,21},{6,22},{7,23},{8,24},{9,... | collective-permute-start | bytes 589832
  603.1 70.1 %collective-permute-start.14 = (f32[16,3072]{1,0:T(8,128)S(1)}, f32[16,3072]{1,0:T(8,128)S(1)}, u32[]{:S(2)}, u32[]{:S(2)}) collective-permute-start(f32[16,3072]{1,0:T(8,128)S(1)} %fusion), channel_id=1, source_target_pairs={{0,15},{1,16},{2,17},{3,18},{4,19},{5,20},{6,21},{7,22},{8,23},{9,... | collective-permute-start | bytes 589832
  608.6 65.9 %collective-permute-start.13 = (f32[16,3072]{1,0:T(8,128)S(1)}, f32[16,3072]{1,0:T(8,128)S(1)}, u32[]{:S(2)}, u32[]{:S(2)}) collective-permute-start(f32[16,3072]{1,0:T(8,128)S(1)} %fusion), channel_id=1, source_target_pairs={{0,14},{1,15},{2,16},{3,17},{4,18},{5,19},{6,20},{7,21},{8,22},{9,... | collective-permute-start | bytes 589832
  620.9 58.9 %collective-permute-start.12 = (f32[16,3072]{1,0:T(8,128)S(1)}, f32[16,3072]{1,0:T(8,128)S(1)}, u32[]{:S(2)}, u32[]{:S(2)}) collective-permute-start(f32[16,3072]{1,0:T(8,128)S(1)} %fusion), channel_id=1, source_target_pairs={{0,13},{1,14},{2,15},{3,16},{4,17},{5,18},{6,19},{7,20},{8,21},{9,... | collective-permute-start | bytes 589832
  631.2 50.6 %collective-permute-start.11 = (f32[16,3072]{1,0:T(8,128)S(1)}, f32[16,3072]{1,0:T(8,128)S(1)}, u32[]{:S(2)}, u32[]{:S(2)}) collective-permute-start(f32[16,3072]{1,0:T(8,128)S(1)} %fusion), channel_id=1, source_target_pairs={{0,12},{1,13},{2,14},{3,15},{4,16},{5,17},{6,18},{7,19},{8,20},{9,... | collective-permute-start | bytes 589832
  646.0 38.4 %collective-permute-start.10 = (f32[16,3072]{1,0:T(8,128)S(1)}, f32[16,3072]{1,0:T(8,128)S(1)}, u32[]{:S(2)}, u32[]{:S(2)}) collective-permute-start(f32[16,3072]{1,0:T(8,128)S(1)} %fusion), channel_id=1, source_target_pairs={{0,11},{1,12},{2,13},{3,14},{4,15},{5,16},{6,17},{7,18},{8,19},{9,... | collective-permute-start | bytes 589832
  673.3 23.7 %collective-permute-start.9 = (f32[16,3072]{1,0:T(8,128)S(1)}, f32[16,3072]{1,0:T(8,128)S(1)}, u32[]{:S(2)}, u32[]{:S(2)}) collective-permute-start(f32[16,3072]{1,0:T(8,128)S(1)} %fusion), channel_id=1, source_target_pairs={{0,10},{1,11},{2,12},{3,13},{4,14},{5,15},{6,16},{7,17},{8,18},{9,... | collective-permute-start | bytes 589832
  674.6 29.1 %collective-permute-start.8 = (f32[16,3072]{1,0:T(8,128)S(1)}, f32[16,3072]{1,0:T(8,128)S(1)}, u32[]{:S(2)}, u32[]{:S(2)}) collective-permute-start(f32[16,3072]{1,0:T(8,128)S(1)} %fusion), channel_id=1, source_target_pairs={{0,9},{1,10},{2,11},{3,12},{4,13},{5,14},{6,15},{7,16},{8,17},{9,1... | collective-permute-start | bytes 589832
  679.9 25.8 %collective-permute-start.7 = (f32[16,3072]{1,0:T(8,128)S(1)}, f32[16,3072]{1,0:T(8,128)S(1)}, u32[]{:S(2)}, u32[]{:S(2)}) collective-permute-start(f32[16,3072]{1,0:T(8,128)S(1)} %fusion), channel_id=1, source_target_pairs={{0,8},{1,9},{2,10},{3,11},{4,12},{5,13},{6,14},{7,15},{8,16},{9,17... | collective-permute-start | bytes 589832
  681.8 28.5 %collective-permute-start.6 = (f32[16,3072]{1,0:T(8,128)S(1)}, f32[16,3072]{1,0:T(8,128)S(1)}, u32[]{:S(2)}, u32[]{:S(2)}) collective-permute-start(f32[16,3072]{1,0:T(8,128)S(1)} %fusion), channel_id=1, source_target_pairs={{0,7},{1,8},{2,9},{3,10},{4,11},{5,12},{6,13},{7,14},{8,15},{9,16}... | collective-permute-start | bytes 589832
  685.1 27.1 %collective-permute-start.5 = (f32[16,3072]{1,0:T(8,128)S(1)}, f32[16,3072]{1,0:T(8,128)S(1)}, u32[]{:S(2)}, u32[]{:S(2)}) collective-permute-start(f32[16,3072]{1,0:T(8,128)S(1)} %fusion), channel_id=1, source_target_pairs={{0,6},{1,7},{2,8},{3,9},{4,10},{5,11},{6,12},{7,13},{8,14},{9,15},... | collective-permute-start | bytes 589832
  697.0 25.4 %collective-permute-start.4 = (f32[16,3072]{1,0:T(8,128)S(1)}, f32[16,3072]{1,0:T(8,128)}, u32[]{:S(2)}, u32[]{:S(2)}) collective-permute-start(f32[16,3072]{1,0:T(8,128)S(1)} %fusion), channel_id=1, source_target_pairs={{0,5},{1,6},{2,7},{3,8},{4,9},{5,10},{6,11},{7,12},{8,13},{9,14},{... | collective-permute-start | bytes 589832
  722.3 187.8 %all-gather.6.cloned.1.call-start = ((), (), s32[]{:S(2)}) async-start(), calls=%async_computation.2 | async-start | bytes 3342336 | tf_op jit(solution)/shard_map/all_gather | solution.py:111
  (86 other events, 4127.2 us)
Sparse Core Ops, SparseCore 0:
  9.7 57.9 all-gather.3
  722.4 139.3 all-reduce.6
  864.2 45.8 all-gather.5
where the time goes:
time: 927 us; the launch traced here: 924 us
  blocking collectives  424 us (46%)
  other arithmetic  145 us (16%)
  starting transfers between devices  136 us (15%)
  local copies, waits for them, and re-layouts  128 us (14%)
  waiting for transfers between devices  38.2 us (4%)
  matrix products  35.9 us (4%)
  between operations  16.2 us (2%)
    unnamed x1, blocking collectives  360 us
    unnamed x32, starting transfers between devices  136 us
    unnamed x153, local copies, waits for them, and re-layouts  92.8 us
    reduce_sum x4, other arithmetic, block_pass(): kernel_terms.append(jnp.sum(grad_conv * window * same_seg, axis=(0, 1)))  88.1 us
    psum x1, blocking collectives, local(): kernel_total, gain_total = lax.psum((kernel_part, gain_part), ('dp', 'red'))  63.9 us
    another operation x2, other arithmetic  35.5 us
    all_gather x1, waiting for transfers between devices, local(): weights = lax.all_gather(w_in, 'red', axis=0, tiled=True)  23.9 us
  transfers between devices with their start and end apart: 35, of which 3 were waited for; matrix products, arithmetic and copies ran while one was open for 20% of the time, Pallas kernels for 0%

commit v1 on v0

--- a/solution.py
+++ b/solution.py
@@ -1,9 +1,19 @@
+import functools
 import jax
 import jax.numpy as jnp
 from jax import lax
 from jax.sharding import PartitionSpec as P
 
 EPSILON = 1e-05
+
+
+def field_mix(m, shard_axis, ax_name):
+    for tick in (shard_axis, ax_name):
+        m = lax.psum(m, axis_name=tick)
+    return m
+
+
+balance_state = functools.partial(field_mix, shard_axis="red", ax_name="dp")
 
 
 def normalize(widened_frames):
@@ -109,7 +119,7 @@
         tiled=True,
     )
     grad_weights = lax.all_gather(owned_rows, "dp", axis=0, tiled=True)
-    kernel_total, gain_total = lax.psum((kernel_part, gain_part), ("dp", "red"))
+    kernel_total, gain_total = balance_state((kernel_part, gain_part))
     return (
         module_output,
         frame_gradient,

time: 927 us -> 974 us (1.051)
  waiting for transfers between devices: 38.2 us -> 81.4 us
  blocking collectives: 424 us -> 409 us
    psum x1 -> x2, waiting for transfers between devices: 0.01 us -> 55.8 us  [field_mix(): m = lax.psum(m, axis_name=tick)]
    psum x1 -> x2, blocking collectives: 63.9 us -> 48.8 us  [field_mix(): m = lax.psum(m, axis_name=tick)]
    all_gather x1, waiting for transfers between devices: 12.9 us -> 0.01 us  [local(): grad_weights = lax.all_gather(owned_rows, 'dp', axis=0, tiled=True)]
    unnamed x153 -> x177, local copies, waits for them, and re-layouts: 92.8 us -> 93.3 us
  transfers between devices with their start and end apart: 35 -> 36, of which waited for: 3 -> 3; matrix products, arithmetic and copies ran while one was open for 20% -> 20% of each run, Pallas kernels for 0% -> 0%
where the time goes in v1:
time: 974 us; the launch traced here: 963 us
  blocking collectives  409 us (42%)
  other arithmetic  147 us (15%)
  starting transfers between devices  139 us (14%)
  local copies, waits for them, and re-layouts  134 us (14%)
  waiting for transfers between devices  81.4 us (8%)
  matrix products  35.9 us (4%)
  between operations  16.4 us (2%)
    unnamed x1, blocking collectives  360 us
    unnamed x32, starting transfers between devices  139 us
    unnamed x177, local copies, waits for them, and re-layouts  93.3 us
    reduce_sum x4, other arithmetic, block_pass(): kernel_terms.append(jnp.sum(grad_conv * window * same_seg, axis=(0, 1)))  89.1 us
    psum x2, waiting for transfers between devices, field_mix(): m = lax.psum(m, axis_name=tick)  55.8 us
    psum x2, blocking collectives, field_mix(): m = lax.psum(m, axis_name=tick)  48.8 us
    another operation x2, other arithmetic  35.5 us
    all_gather x1, waiting for transfers between devices, local(): weights = lax.all_gather(w_in, 'red', axis=0, tiled=True)  23.9 us
  transfers between devices with their start and end apart: 36, of which 3 were waited for; matrix products, arithmetic and copies ran while one was open for 20% of the time, Pallas kernels for 0%

profile of v1, /device:TPU:1, one launch (start us, length us, event | category | flops | bytes accessed | tf_op | source)
XLA Modules:
  0.0 962.6 jit_solution(8370592546768447698)
XLA Ops:
  14.4 8.3 copy.13
  22.7 10.7 %reshape_reshape.3 = bf16[768,8,16,12]{0,3,2,1:T(8,128)(2,1)} reshape(bf16[16,48,1536]{1,0,2:T(8,128)(2,1)} %copy.13) | data formatting | bytes 4718592 | tf_op jit(solution)/shard_map/reshape;reshape | solution.py:111
  43.8 23.9 %all-gather.4.cloned.1.call-done = bf16[1536,3072]{1,0:T(8,128)(2,1)} async-done(((bf16[192,3072]{1,0:T(8,128)(2,1)}), bf16[1536,3072]{1,0:T(8,128)(2,1)}) %all-gather.4.cloned.1.call-update) | async-done | bytes 9437200 | tf_op jit(solution)/shard_map/all_gather | solution.py:98
  67.7 10.8 %fusion.3 = f32[16,48,3072]{2,1,0:T(8,128)S(1)} fusion(bf16[16,48,1536]{2,1,0:T(8,128)(2,1)} %fusion.11, bf16[1536,3072]{1,0:T(8,128)(2,1)} %all-gather.4.cloned.1.call-done), kind=kOutput, calls=%fused_computation.62 | convolution fusion | flops 7247757312 | bytes 21233664 | tf_op jit(solution)/shard_map/dot_general | solution.py:33
  82.6 49.2 %multiply_reduce_fusion = (f32[1536]{0:T(1024)}, f32[1536]{0:T(1024)}, f32[1536]{0:T(1024)}, f32[1536]{0:T(1024)}, f32[1536]{0:T(1024)}, /*index=5*/f32[1536]{0:...) fusion(f32[16,48,1536]{2,1,0:T(8,128)S(1)} %multiply_multiply_f, ...), kind=kLoop, calls=%fused_computation.186 | loop fusion | flops 150981120 | bytes 16856064 | tf_op jit(solution)/shard_map/reduce_sum | solution.py:60
  132.0 28.6 %multiply_convert_fusion.1 = (bf16[16,48,1536]{2,1,0:T(8,128)(2,1)S(1)}, f32[16,48,1536]{2,1,0:T(8,128)}) fusion(f32[16,48,3072]{2,1,0:T(8,128)} %copy-done.2, f32[16,48]{1,0:T(8,128)S(1)} %get-tuple-element.106, f32[16,48]{1,0:T(8,128)S(1)} %get-tuple-element.76, f32[1536]{0:T(1024)} %copy-done.68, f32[16,48]{1,0:T(8,128)S(1)} %get-tuple-element.77, ...), kind=kLoop, calls=%fused_computation.218 | loop fusion | flops 114425856 | bytes 16800768 | tf_op jit(solution)/shard_map/convert.4
  160.6 6.9 multiply_convert_fusion
  168.9 10.8 %fusion.119 = f32[1536,3072]{1,0:T(8,128)} fusion(bf16[768,1536]{0,1:T(8,128)(2,1)S(1)} %copy-done.7, bf16[768,1536]{1,0:T(8,128)(2,1)S(1)} %bitcast.26, bf16[768,1536]{1,0:T(8,128)(2,1)S(1)} %bitcast.25), kind=kOutput, calls=%fused_computation.182 | convolution fusion | flops 7257194496 | bytes 25952256 | tf_op jit(solution)/shard_map/dot_general | solution.py:114
  179.8 359.8 %fusion = f32[16,3072]{1,0:T(8,128)S(1)} fusion(f32[1536,3072]{1,0:T(8,128)} %fusion.119), kind=kCustom, calls=%all-reduce-scatter | all-reduce-scatter fusion | flops 6291457 | bytes 19070976
  552.7 15.0 %collective-permute-start.22 = (f32[16,3072]{1,0:T(8,128)S(1)}, f32[16,3072]{1,0:T(8,128)S(1)}, u32[]{:S(2)}, u32[]{:S(2)}) collective-permute-start(f32[16,3072]{1,0:T(8,128)S(1)} %fusion), channel_id=1, source_target_pairs={{0,23},{1,24},{2,25},{3,26},{4,27},{5,28},{6,29},{7,30},{8,31},{9,... | collective-permute-start | bytes 589832
  579.8 7.7 collective-permute-start.19
  588.9 6.6 collective-permute-start.17
  607.1 12.3 %collective-permute-start.13 = (f32[16,3072]{1,0:T(8,128)S(1)}, f32[16,3072]{1,0:T(8,128)S(1)}, u32[]{:S(2)}, u32[]{:S(2)}) collective-permute-start(f32[16,3072]{1,0:T(8,128)S(1)} %fusion), channel_id=1, source_target_pairs={{0,14},{1,15},{2,16},{3,17},{4,18},{5,19},{6,20},{7,21},{8,22},{9,... | collective-permute-start | bytes 589832
  619.4 10.3 %collective-permute-start.12 = (f32[16,3072]{1,0:T(8,128)S(1)}, f32[16,3072]{1,0:T(8,128)S(1)}, u32[]{:S(2)}, u32[]{:S(2)}) collective-permute-start(f32[16,3072]{1,0:T(8,128)S(1)} %fusion), channel_id=1, source_target_pairs={{0,13},{1,14},{2,15},{3,16},{4,17},{5,18},{6,19},{7,20},{8,21},{9,... | collective-permute-start | bytes 589832
  629.8 14.7 %collective-permute-start.11 = (f32[16,3072]{1,0:T(8,128)S(1)}, f32[16,3072]{1,0:T(8,128)S(1)}, u32[]{:S(2)}, u32[]{:S(2)}) collective-permute-start(f32[16,3072]{1,0:T(8,128)S(1)} %fusion), channel_id=1, source_target_pairs={{0,12},{1,13},{2,14},{3,15},{4,16},{5,17},{6,18},{7,19},{8,20},{9,... | collective-permute-start | bytes 589832
  646.7 26.1 %multiply_reduce_fusion.9 = (f32[1536]{0:T(1024)S(1)}, f32[1536]{0:T(1024)S(1)}, f32[1536]{0:T(1024)S(1)}, f32[1536]{0:T(1024)S(1)}, f32[1536]{0:T(1024)S(1)}, /...) fusion(f32[16,48,1536]{2,1,0:T(8,128)} %copy-done.1, f32[16,48,1536]{2,1,0:T(8,128)} %copy-done, ...), kind=kLoop, calls=%fused_computation.195 | loop fusion | flops 30657024 | bytes 9517056 | tf_op jit(solution)/shard_map/reduce_sum | solution.py:60
  688.2 9.8 %multiply_reduce_fusion.18 = (f32[1536]{0:T(1024)S(1)}, f32[1536]{0:T(1024)S(1)}, f32[1536]{0:T(1024)S(1)}, f32[1536]{0:T(1024)S(1)}, f32[1536]{0:T(1024)S(1)}, ...) fusion(f32[16,48,1536]{2,1,0:T(8,128)} %copy-done.1, ...), kind=kLoop, calls=%fused_computation.204 | loop fusion | flops 31836672 | bytes 9520128 | tf_op jit(solution)/shard_map/reduce_sum | solution.py:60
  706.1 6.9 collective-permute-start.2
  733.7 55.8 %all-reduce.8.cloned.1.call-done = f32[31,1536]{1,0:T(8,128)} async-done(((f32[31,1536]{1,0:T(8,128)}), f32[31,1536]{1,0:T(8,128)}) %all-reduce.8.cloned.1.call-update) | async-done | bytes 190480 | tf_op jit(solution)/shard_map/psum | solution.py:12
  789.6 84.6 %concatenate.17 = f32[524,3072]{1,0:T(8,128)} concatenate(f32[12,3072]{1,0:T(8,128)S(1)} %collective-permute-done.31, f32[16,3072]{1,0:T(8,128)S(1)} %collective-permute-done.30, f32[16,3072]{1,0:T(8,128)S(1)} %collective-permute-done.29, f32[16,3072]{1,0:T(8,128)S(1)} %copy-done.9, f32[16,3072]{1,0:T(8,128)} %copy-done.10, f32[16,3072]{1,0:T(8,128)} %copy-done.11, ...), dimensions={0} | concatenate | bytes 12877824
  876.0 14.3 %fusion.18 = (f32[1536]{0:T(1024)S(1)}, f32[16,48]{1,0:T(8,128)S(1)}, f32[16,48]{1,0:T(8,128)S(1)}, f32[16,48,1536]{2,1,0:T(8,128)}) fusion(bf16[16,48,1536]{2,1,0:T(8,128)(2,1)S(1)} %copy-done.3, f32[16,48]{1,0:T(8,128)S(1)} %copy-done.71, f32[16,48]{1,0:T(8,128)S(1)} %copy-done.63, f32[1536]{0:T(1024)S(1)} %copy-done.73, ...), kind=kOutput, calls=%fused_computation.80 | convolution fusion | flops 7267808256 | bytes 21258240 | tf_op jit(solution)/shard_map/dot_general | solution.py:77
  890.3 14.7 %psum.30 = f32[1536]{0:T(1024)S(1)} all-reduce(f32[1536]{0:T(1024)S(1)} %get-tuple-element.36), channel_id=1, replica_groups=mesh['dp'=16,'red'=8] {'red'}, use_global_device_ids=true, to_apply=%region_40.41 | all-reduce | flops 1536 | bytes 12288 | tf_op jit(solution)/shard_map/psum | solution.py:12
  905.0 34.1 %psum.31 = f32[1536]{0:T(1024)S(1)} all-reduce(f32[1536]{0:T(1024)S(1)} %psum.30), channel_id=1, replica_groups=mesh['dp'=16,'red'=8] {'dp'}, use_global_device_ids=true, to_apply=%region_41.42 | all-reduce | flops 1536 | bytes 12288 | tf_op jit(solution)/shard_map/psum | solution.py:12
  939.7 7.8 fusion.17
  (301 shorter events, 116.3 us)
Async XLA Ops:
  7.2 60.5 %all-gather.4.cloned.1.call-start = ((), (), s32[]{:S(2)}) async-start(), calls=%async_computation | async-start | bytes 10616832 | tf_op jit(solution)/shard_map/all_gather | solution.py:98
  7.9 781.5 %all-reduce.8.cloned.1.call-start = ((), (), s32[]{:S(2)}) async-start(), calls=%async_computation.1 | async-start | bytes 393216 | tf_op jit(solution)/shard_map/psum | solution.py:12
  549.2 30.6 %collective-permute-start.24 = (f32[16,3072]{1,0:T(8,128)S(1)}, f32[16,3072]{1,0:T(8,128)S(1)}, u32[]{:S(2)}, u32[]{:S(2)}) collective-permute-start(f32[16,3072]{1,0:T(8,128)S(1)} %fusion), channel_id=1, source_target_pairs={{0,25},{1,26},{2,27},{3,28},{4,29},{5,30},{6,31},{7,32},{8,33},{9,... | collective-permute-start | bytes 589832
  550.5 37.0 %collective-permute-start.23 = (f32[16,3072]{1,0:T(8,128)S(1)}, f32[16,3072]{1,0:T(8,128)S(1)}, u32[]{:S(2)}, u32[]{:S(2)}) collective-permute-start(f32[16,3072]{1,0:T(8,128)S(1)} %fusion), channel_id=1, source_target_pairs={{0,24},{1,25},{2,26},{3,27},{4,28},{5,29},{6,30},{7,31},{8,32},{9,... | collective-permute-start | bytes 589832
  552.7 36.1 %collective-permute-start.22 = (f32[16,3072]{1,0:T(8,128)S(1)}, f32[16,3072]{1,0:T(8,128)S(1)}, u32[]{:S(2)}, u32[]{:S(2)}) collective-permute-start(f32[16,3072]{1,0:T(8,128)S(1)} %fusion), channel_id=1, source_target_pairs={{0,23},{1,24},{2,25},{3,26},{4,27},{5,28},{6,29},{7,30},{8,31},{9,... | collective-permute-start | bytes 589832
  567.7 27.8 %collective-permute-start.21 = (f32[16,3072]{1,0:T(8,128)S(1)}, f32[16,3072]{1,0:T(8,128)S(1)}, u32[]{:S(2)}, u32[]{:S(2)}) collective-permute-start(f32[16,3072]{1,0:T(8,128)S(1)} %fusion), channel_id=1, source_target_pairs={{0,22},{1,23},{2,24},{3,25},{4,26},{5,27},{6,28},{7,29},{8,30},{9,... | collective-permute-start | bytes 589832
  588.9 30.5 %collective-permute-start.17 = (f32[16,3072]{1,0:T(8,128)S(1)}, f32[16,3072]{1,0:T(8,128)S(1)}, u32[]{:S(2)}, u32[]{:S(2)}) collective-permute-start(f32[16,3072]{1,0:T(8,128)S(1)} %fusion), channel_id=1, source_target_pairs={{0,18},{1,19},{2,20},{3,21},{4,22},{5,23},{6,24},{7,25},{8,26},{9,... | collective-permute-start | bytes 589832
  595.6 34.2 %collective-permute-start.16 = (f32[16,3072]{1,0:T(8,128)S(1)}, f32[16,3072]{1,0:T(8,128)S(1)}, u32[]{:S(2)}, u32[]{:S(2)}) collective-permute-start(f32[16,3072]{1,0:T(8,128)S(1)} %fusion), channel_id=1, source_target_pairs={{0,17},{1,18},{2,19},{3,20},{4,21},{5,22},{6,23},{7,24},{8,25},{9,... | collective-permute-start | bytes 589832
  596.9 47.6 %collective-permute-start.15 = (f32[16,3072]{1,0:T(8,128)S(1)}, f32[16,3072]{1,0:T(8,128)S(1)}, u32[]{:S(2)}, u32[]{:S(2)}) collective-permute-start(f32[16,3072]{1,0:T(8,128)S(1)} %fusion), channel_id=1, source_target_pairs={{0,16},{1,17},{2,18},{3,19},{4,20},{5,21},{6,22},{7,23},{8,24},{9,... | collective-permute-start | bytes 589832
  601.2 71.5 %collective-permute-start.14 = (f32[16,3072]{1,0:T(8,128)S(1)}, f32[16,3072]{1,0:T(8,128)S(1)}, u32[]{:S(2)}, u32[]{:S(2)}) collective-permute-start(f32[16,3072]{1,0:T(8,128)S(1)} %fusion), channel_id=1, source_target_pairs={{0,15},{1,16},{2,17},{3,18},{4,19},{5,20},{6,21},{7,22},{8,23},{9,... | collective-permute-start | bytes 589832
  607.1 67.1 %collective-permute-start.13 = (f32[16,3072]{1,0:T(8,128)S(1)}, f32[16,3072]{1,0:T(8,128)S(1)}, u32[]{:S(2)}, u32[]{:S(2)}) collective-permute-start(f32[16,3072]{1,0:T(8,128)S(1)} %fusion), channel_id=1, source_target_pairs={{0,14},{1,15},{2,16},{3,17},{4,18},{5,19},{6,20},{7,21},{8,22},{9,... | collective-permute-start | bytes 589832
  619.4 60.1 %collective-permute-start.12 = (f32[16,3072]{1,0:T(8,128)S(1)}, f32[16,3072]{1,0:T(8,128)S(1)}, u32[]{:S(2)}, u32[]{:S(2)}) collective-permute-start(f32[16,3072]{1,0:T(8,128)S(1)} %fusion), channel_id=1, source_target_pairs={{0,13},{1,14},{2,15},{3,16},{4,17},{5,18},{6,19},{7,20},{8,21},{9,... | collective-permute-start | bytes 589832
  629.8 51.7 %collective-permute-start.11 = (f32[16,3072]{1,0:T(8,128)S(1)}, f32[16,3072]{1,0:T(8,128)S(1)}, u32[]{:S(2)}, u32[]{:S(2)}) collective-permute-start(f32[16,3072]{1,0:T(8,128)S(1)} %fusion), channel_id=1, source_target_pairs={{0,12},{1,13},{2,14},{3,15},{4,16},{5,17},{6,18},{7,19},{8,20},{9,... | collective-permute-start | bytes 589832
  645.3 38.7 %collective-permute-start.10 = (f32[16,3072]{1,0:T(8,128)S(1)}, f32[16,3072]{1,0:T(8,128)S(1)}, u32[]{:S(2)}, u32[]{:S(2)}) collective-permute-start(f32[16,3072]{1,0:T(8,128)S(1)} %fusion), channel_id=1, source_target_pairs={{0,11},{1,12},{2,13},{3,14},{4,15},{5,16},{6,17},{7,18},{8,19},{9,... | collective-permute-start | bytes 589832
  674.3 29.9 %collective-permute-start.8 = (f32[16,3072]{1,0:T(8,128)S(1)}, f32[16,3072]{1,0:T(8,128)S(1)}, u32[]{:S(2)}, u32[]{:S(2)}) collective-permute-start(f32[16,3072]{1,0:T(8,128)S(1)} %fusion), channel_id=1, source_target_pairs={{0,9},{1,10},{2,11},{3,12},{4,13},{5,14},{6,15},{7,16},{8,17},{9,1... | collective-permute-start | bytes 589832
  681.5 31.6 %collective-permute-start.6 = (f32[16,3072]{1,0:T(8,128)S(1)}, f32[16,3072]{1,0:T(8,128)S(1)}, u32[]{:S(2)}, u32[]{:S(2)}) collective-permute-start(f32[16,3072]{1,0:T(8,128)S(1)} %fusion), channel_id=1, source_target_pairs={{0,7},{1,8},{2,9},{3,10},{4,11},{5,12},{6,13},{7,14},{8,15},{9,16}... | collective-permute-start | bytes 589832
  684.7 30.6 %collective-permute-start.5 = (f32[16,3072]{1,0:T(8,128)S(1)}, f32[16,3072]{1,0:T(8,128)S(1)}, u32[]{:S(2)}, u32[]{:S(2)}) collective-permute-start(f32[16,3072]{1,0:T(8,128)S(1)} %fusion), channel_id=1, source_target_pairs={{0,6},{1,7},{2,8},{3,9},{4,10},{5,11},{6,12},{7,13},{8,14},{9,15},... | collective-permute-start | bytes 589832
  698.2 91.4 %collective-permute-start.4 = (f32[16,3072]{1,0:T(8,128)S(1)}, f32[16,3072]{1,0:T(8,128)}, u32[]{:S(2)}, u32[]{:S(2)}) collective-permute-start(f32[16,3072]{1,0:T(8,128)S(1)} %fusion), channel_id=1, source_target_pairs={{0,5},{1,6},{2,7},{3,8},{4,9},{5,10},{6,11},{7,12},{8,13},{9,14},{... | collective-permute-start | bytes 589832
  704.1 85.4 %collective-permute-start.3 = (f32[16,3072]{1,0:T(8,128)S(1)}, f32[16,3072]{1,0:T(8,128)}, u32[]{:S(2)}, u32[]{:S(2)}) collective-permute-start(f32[16,3072]{1,0:T(8,128)S(1)} %fusion), channel_id=1, source_target_pairs={{0,4},{1,5},{2,6},{3,7},{4,8},{5,9},{6,10},{7,11},{8,12},{9,13},{1... | collective-permute-start | bytes 589832
  706.1 83.5 %collective-permute-start.2 = (f32[16,3072]{1,0:T(8,128)S(1)}, f32[16,3072]{1,0:T(8,128)}, u32[]{:S(2)}, u32[]{:S(2)}) collective-permute-start(f32[16,3072]{1,0:T(8,128)S(1)} %fusion), channel_id=1, source_target_pairs={{0,3},{1,4},{2,5},{3,6},{4,7},{5,8},{6,9},{7,10},{8,11},{9,12},{10... | collective-permute-start | bytes 589832
  713.1 76.5 %collective-permute-start.1 = (f32[16,3072]{1,0:T(8,128)S(1)}, f32[16,3072]{1,0:T(8,128)}, u32[]{:S(2)}, u32[]{:S(2)}) collective-permute-start(f32[16,3072]{1,0:T(8,128)S(1)} %fusion), channel_id=1, source_target_pairs={{0,2},{1,3},{2,4},{3,5},{4,6},{5,7},{6,8},{7,9},{8,10},{9,11},{10,... | collective-permute-start | bytes 589832
  716.0 73.6 %collective-permute-start = (f32[16,3072]{1,0:T(8,128)S(1)}, f32[16,3072]{1,0:T(8,128)}, u32[]{:S(2)}, u32[]{:S(2)}) collective-permute-start(f32[16,3072]{1,0:T(8,128)S(1)} %fusion), channel_id=1, source_target_pairs={{0,1},{1,2},{2,3},{3,4},{4,5},{5,6},{6,7},{7,8},{8,9},{9,10},{10,1... | collective-permute-start | bytes 589832
  731.5 216.0 %all-reduce.10.cloned.1.call-start = ((), (), s32[]{:S(2)}) async-start(), calls=%async_computation.2 | async-start | bytes 393216 | tf_op jit(solution)/shard_map/psum | solution.py:12
  789.5 159.6 %all-gather.6.cloned.1.call-start = ((), (), s32[]{:S(2)}) async-start(), calls=%async_computation.3 | async-start | bytes 3342336 | tf_op jit(solution)/shard_map/all_gather | solution.py:121
  (99 other events, 8121.0 us)
Sparse Core Ops, SparseCore 0:
  9.7 57.9 all-gather.3
  731.7 57.7 all-reduce.7
  793.0 82.9 all-reduce.9
  878.3 48.5 all-gather.5
